TPU v7x, 256 devices: a whole 4x4x8 slice. The times are simulated.
256 devices in a mesh: half: 2 (over z_hi), bf: 128 (over z_lo, y, x, core).
Axes of the slice: x: 4, y: 4, z: 8 (z_hi: 2, z_lo: 4; z = z_hi * 4 + z_lo), core: 2. Of those that a mesh axis runs over, the one named last changes fastest.
Arguments:
- sources: float32 [2, 32, 1048576], P(None, None, ('half', 'bf')), may hold values from -6 to 6
- coarse_in: bfloat16 [2, 4096, 64, 256], P(None, ('half', 'bf')), may hold values from -0.25 to 0.25
- coarse_mix_in: bfloat16 [2, 256, 1024, 512], P(None, ('half', 'bf')), may hold values from -0.125 to 0.125
- coarse_mix_out: bfloat16 [2, 256, 512, 1024], P(None, ('half', 'bf')), may hold values from -0.1875 to 0.1875
- coarse_out: bfloat16 [2, 4096, 64, 256], P(None, ('half', 'bf')), may hold values from -0.5 to 0.5
- fine_in: bfloat16 [2, 4096, 64, 256], P(None, ('half', 'bf')), may hold values from -0.25 to 0.25
- fine_mix_in: bfloat16 [2, 256, 2, 512, 256], P(None, ('half', 'bf')), may hold values from -0.1875 to 0.1875
- fine_mix_out: bfloat16 [2, 256, 2, 256, 512], P(None, ('half', 'bf')), may hold values from -0.25 to 0.25
- fine_out: bfloat16 [2, 4096, 64, 256], P(None, ('half', 'bf')), may hold values from -0.5 to 0.5
- ranks: int32 [4, 4096], P(None, ('half', 'bf')), may hold values from 16 to 64, as said below
Outputs:
- product: float32 [2, 32, 1048576], P(None, None, ('half', 'bf'))
Inputs may be any that keep to these rules, and one draw needn't show every extreme that they name: Each of the four rows of ranks reaches both ends of the range.
All inputs are finite; a program needn't handle non-finite values.
Results may differ from a plain program's by a relative error of at most 0.0057.
Values may be sent and summed in bfloat16 or wider, within the bound.
A program may use at most 64 MiB of HBM per device.

v0:
```python
from functools import partial

import jax
import jax.numpy as jnp
from jax import lax
from jax.sharding import PartitionSpec as P


def partner(block, axis, apart):
    count = lax.axis_size(axis)
    route = []
    for low in range(count):
        high = low | 1 << apart
        if high != low and high < count:
            route += [(low, high), (high, low)]
    return lax.ppermute(block, axis, route)


def halves(array):
    return (array[0], array[1])


def complex_product(spec, left, right, where):
    contract = partial(jnp.einsum, spec, preferred_element_type=jnp.float32)
    left_real, left_imag = left
    right_real, right_imag = right
    real_part = contract(left_real, right_real) - contract(left_imag, right_imag)
    imag_part = contract(left_real, right_imag) + contract(left_imag, right_real)
    return jnp.stack([real_part, imag_part], axis=where)


def local(
    sources,
    coarse_in,
    coarse_mix_in,
    coarse_mix_out,
    coarse_out,
    fine_in,
    fine_mix_in,
    fine_mix_out,
    fine_out,
    ranks,
):
    width = lax.axis_size("bf")
    vectors = sources.shape[1]
    leaf_count = coarse_in.shape[1]
    rank_cap = coarse_in.shape[2]
    leaf_len = coarse_in.shape[3]
    halfway = leaf_count // 2
    links = coarse_mix_in.shape[3] // width
    fine_links = fine_mix_in.shape[4] // width
    narrow = sources.astype(jnp.bfloat16).reshape(2, vectors, leaf_count, leaf_len)
    keeper = (jnp.arange(rank_cap)[None, None, :] < ranks[:, :, None]).astype(jnp.float32)
    coarse_coef = complex_product("nsl,skl->nsk", halves(narrow), halves(coarse_in), 0)
    coarse_coef = (coarse_coef * keeper[0]).astype(jnp.bfloat16)
    fine_coef = complex_product("nsl,skl->nsk", halves(narrow), halves(fine_in), 0)
    fine_coef = (fine_coef * keeper[2]).astype(jnp.bfloat16)
    coarse_mix = coarse_mix_in[:, 0].reshape(2, leaf_count * rank_cap, width, links)
    coarse_send = complex_product(
        "nk,kjc->jnc",
        halves(coarse_coef.reshape(2, vectors, leaf_count * rank_cap)),
        halves(coarse_mix),
        1,
    )
    coarse_flat = coarse_send.astype(jnp.bfloat16).reshape(width, -1)
    fine_mix = fine_mix_in[:, 0].reshape(2, 2, halfway * rank_cap, width, fine_links)
    fine_send = complex_product(
        "nik,ikjc->jinc",
        halves(fine_coef.reshape(2, vectors, 2, halfway * rank_cap)),
        halves(fine_mix),
        2,
    )
    fine_flat = fine_send.astype(jnp.bfloat16).reshape(width, -1)
    crossed = partner(coarse_flat, "half", 0)
    coarse_recv = lax.all_to_all(crossed, "bf", split_axis=0, concat_axis=0, tiled=True)
    fine_recv = lax.all_to_all(fine_flat, "bf", split_axis=0, concat_axis=0, tiled=True)
    coarse_got = coarse_recv.reshape(width, 2, vectors, links)
    back_mix = coarse_mix_out[:, 0].reshape(2, width, links, leaf_count * rank_cap)
    coarse_back = complex_product(
        "cnq,cqk->nk", (coarse_got[:, 0], coarse_got[:, 1]), halves(back_mix), 0
    )
    coarse_back = (coarse_back.reshape(2, vectors, leaf_count, rank_cap) * keeper[1]).astype(
        jnp.bfloat16
    )
    coarse_part = complex_product("nsk,skl->nsl", halves(coarse_back), halves(coarse_out), 0)
    fine_got = fine_recv.reshape(width, 2, 2, vectors, fine_links)
    fine_back_mix = fine_mix_out[:, 0].reshape(2, 2, width, fine_links, halfway * rank_cap)
    fine_back = complex_product(
        "cinq,icqk->nik", (fine_got[:, :, 0], fine_got[:, :, 1]), halves(fine_back_mix), 0
    )
    fine_back = jnp.flip(fine_back, 2).reshape(2, vectors, leaf_count, rank_cap)
    fine_back = (fine_back * keeper[3]).astype(jnp.bfloat16)
    fine_part = complex_product("nsk,skl->nsl", halves(fine_back), halves(fine_out), 0)
    return (coarse_part + fine_part).reshape(2, vectors, leaf_count * leaf_len)


def solution(mesh):
    return jax.shard_map(
        local,
        mesh=mesh,
        in_specs=(
            P(None, None, ("half", "bf")),
            P(None, ("half", "bf"), None, None),
            P(None, ("half", "bf"), None, None),
            P(None, ("half", "bf"), None, None),
            P(None, ("half", "bf"), None, None),
            P(None, ("half", "bf"), None, None),
            P(None, ("half", "bf"), None, None, None),
            P(None, ("half", "bf"), None, None, None),
            P(None, ("half", "bf"), None, None),
            P(None, ("half", "bf")),
        ),
        out_specs=P(None, None, ("half", "bf")),
        check_vma=False,
    )
```

profile of v0, /device:TPU:1, one launch (start us, length us, event | category | flops | bytes accessed | tf_op | source)
XLA Modules:
  0.0 71.6 jit_solution(5113216058518073555)
XLA Ops:
  0.0 1.4 %convert_element_type.35 = bf16[2,32,4096]{2,1,0:T(8,128)(2,1)S(1)} convert(f32[2,32,4096]{2,1,0:T(8,128)} %param.10) | non-fusion elementwise | flops 262144 | bytes 1572864 | tf_op jit(solution)/shard_map/convert_element_type | solution.py:52
  2.1 0.6 copy-done.7
  6.0 0.5 copy.97
  7.0 0.5 copy.101
  9.0 0.6 reduce.1
  9.7 0.6 reshape.102
  10.3 13.8 %all-to-all-start.1 = ((bf16[128,2,128]{2,1,0:T(2,128)(2,1)}), bf16[128,2,128]{2,1,0:T(2,128)(2,1)S(1)}, u32[]{:S(2)}, u32[]{:S(2)}) async-start(bf16[128,2,128]{2,1,0:T(2,128)(2,1)} %reshape.102), calls=%async_computation.1 | async-start | bytes 131072 | tf_op jit(solution)/shard_map/all_to_all | solution.py:76
  24.6 1.7 %fusion.90 = (bf16[1,1,1024,512]{3,2,1,0:T(8,128)(2,1)S(1)}, bf16[1,1,1024,512]{3,2,1,0:T(8,128)(2,1)S(1)}) fusion(bf16[2,1,1024,512]{3,2,1,0:T(8,128)(2,1)} %param.12), kind=kLoop, calls=%fused_computation.131 | loop fusion | bytes 4194304 | tf_op jit(solution)/shard_map/slice | solution.py:20
  27.3 1.0 %copy.71 = bf16[1024,128,4]{1,0,2:T(8,128)(2,1)S(1)} copy(bf16[1024,128,4]{0,2,1:T(4,128)(2,1)S(1)} %squeeze.97) | data formatting | bytes 2097152 | tf_op jit(solution)/shard_map/squeeze | solution.py:20
  28.3 0.5 copy.73
  29.2 1.0 %copy.74 = bf16[1024,128,4]{1,0,2:T(8,128)(2,1)S(1)} copy(bf16[1024,128,4]{0,2,1:T(4,128)(2,1)S(1)} %squeeze.99) | data formatting | bytes 2097152 | tf_op jit(solution)/shard_map/squeeze | solution.py:20
  31.5 4.3 %collective-permute-start = (bf16[128,256]{0,1:T(8,128)(2,1)S(1)}, bf16[128,256]{0,1:T(8,128)(2,1)S(1)}, u32[]{:S(2)}, u32[]{:S(2)}) collective-permute-start(bf16[128,256]{0,1:T(8,128)(2,1)S(1)} %bitcast.235), channel_id=1, source_target_pairs={{0,128},{128,0},{1,129},{129,1},{2,130},{130,2},{3,131},{131,3},{4... | collective-permute-start | bytes 196616 | tf_op jit(solution)/shard_map/ppermute | solution.py:16
  35.8 1.1 %fusion.89 = (bf16[1,1,512,1024]{3,2,1,0:T(8,128)(2,1)S(1)}, bf16[1,1,512,1024]{3,2,1,0:T(8,128)(2,1)}) fusion(bf16[2,1,512,1024]{3,2,1,0:T(8,128)(2,1)S(1)} %copy-done.2), kind=kLoop, calls=%fused_computation.130 | loop fusion | bytes 4194304 | tf_op jit(solution)/shard_map/slice | solution.py:20
  37.0 0.5 copy.113
  37.5 0.5 copy.110
  38.5 1.5 %squeeze.101 = bf16[128,4,1024]{2,1,0:T(4,128)(2,1)S(1)} reshape(bf16[1,1,512,1024]{3,2,1,0:T(8,128)(2,1)} %get-tuple-element.6) | data formatting | bytes 2097152 | tf_op jit(solution)/shard_map/squeeze | solution.py:20
  40.0 0.6 reduce
  40.7 0.6 reshape.100
  41.4 12.4 %all-to-all-start = ((bf16[128,2,128]{2,1,0:T(2,128)(2,1)}), bf16[128,2,128]{2,1,0:T(2,128)(2,1)S(1)}, u32[]{:S(2)}, u32[]{:S(2)}) async-start(bf16[128,2,128]{2,1,0:T(2,128)(2,1)} %reshape.100), calls=%async_computation | async-start | bytes 131072 | tf_op jit(solution)/shard_map/all_to_all | solution.py:75
  55.1 0.7 %rev.4 = f32[2,32,2,512]{3,1,2,0:T(8,128)} reverse(f32[2,32,2,512]{3,1,2,0:T(8,128)S(1)} %pad_maximum_fusion), dimensions={2} | reverse | bytes 524288 | tf_op jit(solution)/shard_map/jit(_flip)/rev | solution.py:91
  55.8 1.2 %copy.117 = f32[2,32,2,512]{3,2,1,0:T(2,128)S(1)} copy(f32[2,32,2,512]{3,1,2,0:T(8,128)} %rev.4) | data formatting | bytes 524288 | tf_op jit(solution)/shard_map/jit(_flip)/rev | solution.py:91
  56.9 1.1 %reshape.83 = f32[2,32,16,64]{3,2,1,0:T(8,128)} reshape(f32[2,32,2,512]{3,2,1,0:T(2,128)S(1)} %copy.117) | data formatting | bytes 524288 | tf_op jit(solution)/shard_map/reshape | solution.py:91
  58.0 1.2 %fusion.53 = bf16[2,32,16,64]{3,1,2,0:T(8,128)(2,1)S(1)} fusion(f32[2,32,16,64]{3,2,1,0:T(8,128)} %reshape.83, f32[16,64]{1,0:T(8,128)S(1)} %get-tuple-element.23), kind=kLoop, calls=%fused_computation.78 | loop fusion | flops 131072 | bytes 397312 | tf_op jit(solution)/shard_map/convert_element_type | solution.py:92
  59.9 1.0 %fusion.1 = f32[32,16,256]{2,0,1:T(8,128)} fusion(f32[16,32,256]{2,1,0:T(8,128)S(1)} %fusion.33, bf16[2,16,64,256]{3,2,1,0:T(8,128)(2,1)S(1)} %copy-done, bf16[2,32,16,64]{3,1,2,0:T(8,128)(2,1)S(1)} %fusion.53), kind=kOutput, calls=%fused_computation.3 | convolution fusion | flops 16908288 | bytes 1703936 | tf_op jit(solution)/shard_map/nsk,skl->nsl/dot_general | solution.py:27
  61.3 0.9 %stack.100 = f32[1,32,4096]{2,1,0:T(8,128)} reshape(f32[32,16,256]{2,1,0:T(8,128)S(1)} %copy.120) | data formatting | bytes 1048576 | tf_op jit(solution)/shard_map/stack | solution.py:29
  62.5 0.9 %stack.99 = f32[1,32,4096]{2,1,0:T(8,128)} reshape(f32[32,16,256]{2,1,0:T(8,128)S(1)} %copy.119) | data formatting | bytes 1048576 | tf_op jit(solution)/shard_map/stack | solution.py:29
  64.0 0.7 convolution_bitcast_fusion.6
  64.7 0.7 convolution_bitcast_fusion.4
  65.3 0.7 fusion.8
  66.0 0.7 fusion.9
  68.2 0.9 %stack.88 = f32[1,32,4096]{2,1,0:T(8,128)} reshape(f32[32,16,256]{2,1,0:T(8,128)S(1)} %copy.89) | data formatting | bytes 1048576 | tf_op jit(solution)/shard_map/stack | solution.py:29
  70.5 1.1 %maximum_add_fusion = f32[2,32,4096]{2,1,0:T(8,128)} fusion(f32[1,32,4096]{2,1,0:T(8,128)S(1)} %copy-done.6, f32[1,32,4096]{2,1,0:T(8,128)S(1)} %stack.87, f32[1,32,4096]{2,1,0:T(8,128)S(1)} %copy-done.4, f32[1,32,4096]{2,1,0:T(8,128)S(1)} %copy-done.5), kind=kLoop, calls=%fused_computation.42 | loop fusion | flops 786432 | bytes 3145728 | tf_op jit(solution)/shard_map/add | solution.py:94
  (101 shorter events, 15.6 us)
Async XLA Ops:
  0.0 1.5 %copy-start.8 = (bf16[2,16,64,256]{3,2,1,0:T(8,128)(2,1)S(1)}, bf16[2,16,64,256]{3,2,1,0:T(8,128)(2,1)}, u32[]{:S(2)}) copy-start(bf16[2,16,64,256]{3,2,1,0:T(8,128)(2,1)} %param.15) | copy-start | bytes 3145732
  1.4 1.3 %copy-start.7 = (bf16[2,16,64,256]{3,2,1,0:T(8,128)(2,1)S(1)}, bf16[2,16,64,256]{3,2,1,0:T(8,128)(2,1)}, u32[]{:S(2)}) copy-start(bf16[2,16,64,256]{3,2,1,0:T(8,128)(2,1)} %param.11) | copy-start | bytes 3145732
  1.5 1.6 %copy-start.11 = (s32[4,16]{1,0:T(4,128)S(1)}, s32[4,16]{1,0:T(4,128)}, u32[]{:S(2)}) copy-start(s32[4,16]{1,0:T(4,128)} %param.19) | copy-start | bytes 772
  4.2 1.2 %copy-start.9 = (bf16[2,1,2,512,256]{4,3,2,1,0:T(8,128)(2,1)S(1)}, bf16[2,1,2,512,256]{4,3,2,1,0:T(8,128)(2,1)}, u32[]{:S(2)}) copy-start(bf16[2,1,2,512,256]{4,3,2,1,0:T(8,128)(2,1)} %param.16) | copy-start | bytes 3145732
  10.3 31.0 %all-to-all-start.1 = ((bf16[128,2,128]{2,1,0:T(2,128)(2,1)}), bf16[128,2,128]{2,1,0:T(2,128)(2,1)S(1)}, u32[]{:S(2)}, u32[]{:S(2)}) async-start(bf16[128,2,128]{2,1,0:T(2,128)(2,1)} %reshape.102), calls=%async_computation.1 | async-start | bytes 131072 | tf_op jit(solution)/shard_map/all_to_all | solution.py:76
  30.5 5.3 %copy-start.2 = (bf16[2,1,512,1024]{3,2,1,0:T(8,128)(2,1)S(1)}, bf16[2,1,512,1024]{3,2,1,0:T(8,128)(2,1)}, u32[]{:S(2)}) copy-start(bf16[2,1,512,1024]{3,2,1,0:T(8,128)(2,1)} %param.13) | copy-start | bytes 6291460
  31.5 5.5 %copy-start.10 = (bf16[2,1,2,256,512]{4,3,2,1,0:T(8,128)(2,1)S(1)}, bf16[2,1,2,256,512]{4,3,2,1,0:T(8,128)(2,1)}, u32[]{:S(2)}) copy-start(bf16[2,1,2,256,512]{4,3,2,1,0:T(8,128)(2,1)} %param.17) | copy-start | bytes 3145732
  31.5 8.5 %collective-permute-start = (bf16[128,256]{0,1:T(8,128)(2,1)S(1)}, bf16[128,256]{0,1:T(8,128)(2,1)S(1)}, u32[]{:S(2)}, u32[]{:S(2)}) collective-permute-start(bf16[128,256]{0,1:T(8,128)(2,1)S(1)} %bitcast.235), channel_id=1, source_target_pairs={{0,128},{128,0},{1,129},{129,1},{2,130},{130,2},{3,131},{131,3},{4... | collective-permute-start | bytes 196616 | tf_op jit(solution)/shard_map/ppermute | solution.py:16
  41.4 22.4 %all-to-all-start = ((bf16[128,2,128]{2,1,0:T(2,128)(2,1)}), bf16[128,2,128]{2,1,0:T(2,128)(2,1)S(1)}, u32[]{:S(2)}, u32[]{:S(2)}) async-start(bf16[128,2,128]{2,1,0:T(2,128)(2,1)} %reshape.100), calls=%async_computation | async-start | bytes 131072 | tf_op jit(solution)/shard_map/all_to_all | solution.py:75
  55.0 4.3 %copy-start = (bf16[2,16,64,256]{3,2,1,0:T(8,128)(2,1)S(1)}, bf16[2,16,64,256]{3,2,1,0:T(8,128)(2,1)}, u32[]{:S(2)}) copy-start(bf16[2,16,64,256]{3,2,1,0:T(8,128)(2,1)} %param.18) | copy-start | bytes 3145732
  60.9 1.2 %copy-start.3 = (f32[32,16,256]{2,0,1:T(8,128)S(1)}, f32[32,16,256]{2,0,1:T(8,128)}, u32[]{:S(2)}) copy-start(f32[32,16,256]{2,0,1:T(8,128)} %fusion.1) | copy-start | bytes 1572868
  66.0 1.2 %copy-start.1 = (bf16[2,16,64,256]{3,2,1,0:T(8,128)(2,1)S(1)}, bf16[2,16,64,256]{3,2,1,0:T(8,128)(2,1)}, u32[]{:S(2)}) copy-start(bf16[2,16,64,256]{3,2,1,0:T(8,128)(2,1)} %param.14) | copy-start | bytes 3145732
  69.1 1.0 %copy-start.4 = (f32[1,32,4096]{2,1,0:T(8,128)S(1)}, f32[1,32,4096]{2,1,0:T(8,128)}, u32[]{:S(2)}) copy-start(f32[1,32,4096]{2,1,0:T(8,128)} %stack.100) | copy-start | bytes 1572868
  69.1 1.2 %copy-start.5 = (f32[1,32,4096]{2,1,0:T(8,128)S(1)}, f32[1,32,4096]{2,1,0:T(8,128)}, u32[]{:S(2)}) copy-start(f32[1,32,4096]{2,1,0:T(8,128)} %stack.99) | copy-start | bytes 1572868
  69.3 1.2 %copy-start.6 = (f32[1,32,4096]{2,1,0:T(8,128)S(1)}, f32[1,32,4096]{2,1,0:T(8,128)}, u32[]{:S(2)}) copy-start(f32[1,32,4096]{2,1,0:T(8,128)} %stack.88) | copy-start | bytes 1572868
where the time goes:
time: 72.1 us; the launch traced here: 71.6 us
  starting transfers between devices  30.5 us (42%)
  local copies, waits for them, and re-layouts  24.6 us (34%)
  matrix products  10.4 us (14%)
  other arithmetic  5.14 us (7%)
    all_to_all x1, starting transfers between devices, local(): lax.all_to_all(fine_flat, 'bf', split_axis=0, concat_axis=0, tiled=True)  13.8 us
    all_to_all x1, starting transfers between devices, local(): lax.all_to_all(crossed, 'bf', split_axis=0, concat_axis=0, tiled=True)  12.4 us
    slice x17, local copies, waits for them, and re-layouts, halves(): return (array[0], array[1])  6.42 us
    squeeze x12, local copies, waits for them, and re-layouts, halves(): return (array[0], array[1])  6.35 us
    ppermute x1, starting transfers between devices, partner(): return lax.ppermute(block, axis, route)  4.3 us
    unnamed x32, local copies, waits for them, and re-layouts  3.54 us
    another operation x10, local copies, waits for them, and re-layouts, complex_product(): return jnp.stack([real_part, imag_part], axis=where)  3.26 us
    dot_general x8, matrix products, complex_product(): contract(left_imag, right_imag)  3.2 us
  transfers between devices with their start and end apart: 3, of which 1 were waited for; matrix products, arithmetic and copies ran while one was open for 31% of the time, Pallas kernels for 0%

commit v1 on v0

v1 whole, which is shorter than its diff:
```python
import functools

import jax
import jax.numpy as jnp
from jax import lax
from jax.experimental import pallas as pl
from jax.experimental.pallas import tpu as pltpu
from jax.sharding import PartitionSpec as P

F32 = jnp.float32
BF16 = jnp.bfloat16
MESH = pl.DeviceIdType.MESH
GROUPS = 8
MEMBERS = 16
ROWS = 32
LEAVES = 16
RANK = 64
LEAF = 256
VECTORS = 32
CHUNKS = 4


def dot(left, right):
    return lax.dot_general(left, right, (((1,), (0,)), ((), ())), preferred_element_type=F32)


def dot_t(left, right):
    return lax.dot_general(left, right, (((1,), (1,)), ((), ())), preferred_element_type=F32)


def iota(shape, axis):
    return lax.broadcasted_iota(jnp.int32, shape, axis)


def complex_rows(by_real, by_imag):
    n = VECTORS
    return by_real[:n] - by_imag[n:], by_real[n:] + by_imag[:n]


def kernel(
    sources, coarse_in, coarse_mix_in, coarse_mix_out, coarse_out,
    fine_in, fine_mix_in, fine_mix_out, fine_out, ranks,
    out,
    x_v, ci_v, cmi_v, cmo_v, co_v, fi_v, fmi_v, fmo_v, fo_v, ranks_s,
    regroup, pairs, spread, ccoef, fcoef, cback, fback,
    cs1, cr1, cs2, cr2, fs1, fr1, fs2, fr2, out_v,
    in_sem, send_sem, recv_sem, out_sem,
):
    half = lax.axis_index("half")
    block = lax.axis_index("bf")
    group = block // MEMBERS
    member = block % MEMBERS

    per = LEAVES // CHUNKS
    loads = {}

    def load(name, source, target):
        copy = pltpu.make_async_copy(source, target, in_sem.at[len(loads)])
        copy.start()
        loads[name] = copy

    load("ranks", ranks, ranks_s)
    for c in range(CHUNKS):
        span = pl.ds(c * per, per)
        cols = pl.ds(c * per * LEAF, per * LEAF)
        load(("x", c), sources.at[:, :, cols], x_v.at[:, :, cols])
        load(("ci", c), coarse_in.at[:, span], ci_v.at[:, span])
        load(("fi", c), fine_in.at[:, span], fi_v.at[:, span])
    load("cmi", coarse_mix_in, cmi_v)
    load("fmi", fine_mix_in, fmi_v)
    load("cmo", coarse_mix_out, cmo_v)
    load("fmo", fine_mix_out, fmo_v)
    load("co", coarse_out, co_v)
    load("fo", fine_out, fo_v)

    barrier = pltpu.get_barrier_semaphore()

    def greet(h, b):
        pl.semaphore_signal(barrier, inc=1, device_id=(h, b), device_id_type=MESH)

    for k in range(GROUPS):
        there = (group + k) % GROUPS * MEMBERS + member
        greet(1 - half, there)
        if k:
            greet(half, there)
    for k in range(1, MEMBERS):
        greet(half, group * MEMBERS + (member + k) % MEMBERS)

    def regrouped(row):
        return row // 2 % GROUPS * ROWS + row // (2 * GROUPS) * 2 + row % 2

    rows = iota((256, 256), 0)
    regroup[...] = (regrouped(rows) == iota((256, 256), 1)).astype(F32).astype(BF16)
    rows = iota((256, 512), 0)
    cols = iota((256, 512), 1) // 2
    spread[...] = (regrouped(rows) == cols).astype(F32).astype(BF16)
    pairs[...] = (rows == cols).astype(F32).astype(BF16)

    lane = iota((1, 128), 1)
    low = lane < RANK

    def keep(first, second):
        return lane < jnp.where(low, first, second + RANK)

    loads["ranks"].wait()
    for c in range(CHUNKS):
        for name in ("x", "ci", "fi"):
            loads[name, c].wait()
        for first in range(c * per, (c + 1) * per, 2):
            got = []
            for s in (first, first + 1):
                x = x_v[:, :, s * LEAF : (s + 1) * LEAF].astype(BF16).reshape(2 * VECTORS, LEAF)
                two = (ci_v, fi_v) if s == first else (fi_v, ci_v)
                w = jnp.concatenate([two[0][0, s], two[1][0, s], two[0][1, s], two[1][1, s]], axis=0)
                y = dot_t(x, w)
                re, im = complex_rows(y[:, :128], y[:, 128:])
                which = (0, 2) if s == first else (2, 0)
                kept = keep(ranks_s[which[0], s], ranks_s[which[1], s])
                both = jnp.concatenate([re, im], axis=0)
                got.append(jnp.where(kept, both, 0.0))
            at = pl.ds(first * RANK, 2 * RANK)
            ccoef[:, at] = jnp.where(low, got[0], got[1]).astype(BF16)
            fcoef[:, at] = jnp.where(low, got[1], got[0]).astype(BF16)

    def remote(source, target, which, h, b):
        pltpu.make_async_remote_copy(
            src_ref=source, dst_ref=target, send_sem=send_sem.at[which], recv_sem=recv_sem.at[which],
            device_id=(h, b), device_id_type=MESH,
        ).start()

    def arrived(buffer, which):
        pltpu.make_async_copy(buffer, buffer, recv_sem.at[which]).wait()

    def sent(buffer, which):
        pltpu.make_async_copy(buffer, buffer, send_sem.at[which]).wait()

    loads["cmi"].wait()
    re, im = complex_rows(dot(ccoef[...], cmi_v[0, 0]), dot(ccoef[...], cmi_v[1, 0]))
    send = jnp.concatenate([re, im], axis=0)
    even = iota((1, 512), 1) % 2 == 0
    send = jnp.concatenate([jnp.where(even, send, 0.0), jnp.where(even, 0.0, send)], axis=0).astype(BF16)
    cs1[...] = dot_t(pairs[...], send).astype(BF16).reshape(GROUPS, ROWS, 128)

    pl.semaphore_wait(barrier, 2 * GROUPS - 1 + MEMBERS - 1)
    for k in range(GROUPS):
        there = (group + k) % GROUPS
        remote(cs1.at[there], cr1.at[group], 0, 1 - half, there * MEMBERS + member)

    loads["fmi"].wait()
    fine = []
    for i in range(2):
        left = fcoef[:, i * 512 : (i + 1) * 512]
        parts = []
        for part in range(2):
            order = [leaf ^ 1 for leaf in range(LEAVES // 2)]
            w = jnp.concatenate(
                [fmi_v[part, 0, i, leaf * RANK : (leaf + 1) * RANK, :] for leaf in order], axis=0
            )
            parts.append(dot(left, w))
        fine.extend(complex_rows(*parts))
    send = jnp.concatenate(fine, axis=0)
    fs1[...] = send.T.astype(BF16).reshape(GROUPS, ROWS, 128)
    for k in range(1, GROUPS):
        there = (group + k) % GROUPS
        remote(fs1.at[there], fr1.at[group], 1, half, there * MEMBERS + member)
    pltpu.make_async_copy(fs1.at[group], fr1.at[group], recv_sem.at[1]).start()

    def pass_on(received, outgoing, landing, first, which):
        arrived(received, first)
        rows = received[...].reshape(256, 128)
        outgoing[...] = dot(regroup[...], rows).astype(BF16).reshape(MEMBERS, 2 * GROUPS, 128)
        for k in range(1, MEMBERS):
            there = (member + k) % MEMBERS
            remote(outgoing.at[there], landing.at[member], which, half, group * MEMBERS + there)
        pltpu.make_async_copy(outgoing.at[member], landing.at[member], recv_sem.at[which]).start()

    pass_on(cr1, cs2, cr2, 0, 2)
    pass_on(fr1, fs2, fr2, 1, 3)

    arrived(cr2, 2)
    got = dot(cr2[...].reshape(256, 128).T, spread[...])
    left = jnp.where(even, got[:64], got[64:]).astype(BF16)
    loads["cmo"].wait()
    for at in range(0, 1024, 256):
        re, im = complex_rows(dot(left, cmo_v[0, 0, :, at : at + 256]), dot(left, cmo_v[1, 0, :, at : at + 256]))
        for n in range(2):
            leaf = at // RANK + 2 * n
            kept = keep(ranks_s[1, leaf], ranks_s[1, leaf + 1])
            cols = slice(128 * n, 128 * n + 128)
            cback[0, :, at + 128 * n : at + 128 * n + 128] = jnp.where(kept, re[:, cols], 0.0)
            cback[1, :, at + 128 * n : at + 128 * n + 128] = jnp.where(kept, im[:, cols], 0.0)

    arrived(fr2, 3)
    got = dot(fr2[...].reshape(256, 128).T, regroup[...]).astype(BF16)
    loads["fmo"].wait()
    for i in range(2):
        left = got[i * 64 : i * 64 + 64]
        for at in range(0, 512, 256):
            re, im = complex_rows(
                dot(left, fmo_v[0, 0, i, :, at : at + 256]), dot(left, fmo_v[1, 0, i, :, at : at + 256])
            )
            for n in range(2):
                place = (1 - i) * 512 + at + 128 * n
                leaf = place // RANK
                kept = keep(ranks_s[3, leaf], ranks_s[3, leaf + 1])
                cols = slice(128 * n, 128 * n + 128)
                fback[0, :, place : place + 128] = pltpu.roll(jnp.where(kept, re[:, cols], 0.0), RANK, 1)
                fback[1, :, place : place + 128] = pltpu.roll(jnp.where(kept, im[:, cols], 0.0), RANK, 1)

    loads["co"].wait()
    loads["fo"].wait()
    for first in range(0, LEAVES, 2):
        at = slice(first * RANK, first * RANK + 128)
        cr, ci, fr, fi = cback[0, :, at], cback[1, :, at], fback[0, :, at], fback[1, :, at]
        for s in (first, first + 1):
            if s == first:
                re, im = jnp.where(low, cr, fr), jnp.where(low, ci, fi)
                two = (co_v, fo_v)
            else:
                re, im = jnp.where(low, fr, cr), jnp.where(low, fi, ci)
                two = (fo_v, co_v)
            left = jnp.concatenate(
                [jnp.concatenate([re, -im], axis=1), jnp.concatenate([im, re], axis=1)], axis=0
            ).astype(BF16)
            w = jnp.concatenate([two[0][0, s], two[1][0, s], two[0][1, s], two[1][1, s]], axis=0)
            out_v[:, :, s * LEAF : (s + 1) * LEAF] = dot(left, w).reshape(2, VECTORS, LEAF)
        if first % per == per - 2:
            span = pl.ds((first + 2 - per) * LEAF, per * LEAF)
            pltpu.make_async_copy(out_v.at[:, :, span], out.at[:, :, span], out_sem.at[first // per]).start()

    sent(cs1, 0)
    sent(fs1.at[pl.ds(0, GROUPS - 1)], 1)
    sent(cs2.at[pl.ds(0, MEMBERS - 1)], 2)
    sent(fs2.at[pl.ds(0, MEMBERS - 1)], 3)
    for c in range(CHUNKS):
        span = pl.ds(c * per * LEAF, per * LEAF)
        pltpu.make_async_copy(out_v.at[:, :, span], out.at[:, :, span], out_sem.at[c]).wait()


def local(*args):
    anywhere = pl.BlockSpec(memory_space=pl.ANY)
    shapes = [a.shape for a in args]
    vmem = pltpu.VMEM
    return pl.pallas_call(
        kernel,
        out_shape=jax.ShapeDtypeStruct(shapes[0], F32),
        in_specs=[anywhere] * len(args),
        out_specs=anywhere,
        scratch_shapes=[
            vmem(shapes[0], F32),
            *[vmem(s, BF16) for s in shapes[1:9]],
            pltpu.SMEM(shapes[9], jnp.int32),
            vmem((256, 256), BF16),
            vmem((256, 512), BF16),
            vmem((256, 512), BF16),
            vmem((64, 1024), BF16),
            vmem((64, 1024), BF16),
            vmem((2, 32, 1024), F32),
            vmem((2, 32, 1024), F32),
            *[
                vmem(s, BF16)
                for s in [
                    (GROUPS, ROWS, 128), (GROUPS, ROWS, 128), (MEMBERS, 2 * GROUPS, 128), (MEMBERS, 2 * GROUPS, 128),
                ]
                * 2
            ],
            vmem(shapes[0], F32),
            pltpu.SemaphoreType.DMA((1 + 3 * CHUNKS + 6,)),
            pltpu.SemaphoreType.DMA((4,)),
            pltpu.SemaphoreType.DMA((4,)),
            pltpu.SemaphoreType.DMA((CHUNKS,)),
        ],
        compiler_params=pltpu.CompilerParams(
            collective_id=0, has_side_effects=True, vmem_limit_bytes=40 * 1024 * 1024
        ),
        cost_estimate=pl.CostEstimate(flops=672 * 10**6, bytes_accessed=12 * 2**20, transcendentals=0),
    )(*args)


def solution(mesh):
    return jax.shard_map(
        local,
        mesh=mesh,
        in_specs=(
            P(None, None, ("half", "bf")),
            P(None, ("half", "bf"), None, None),
            P(None, ("half", "bf"), None, None),
            P(None, ("half", "bf"), None, None),
            P(None, ("half", "bf"), None, None),
            P(None, ("half", "bf"), None, None),
            P(None, ("half", "bf"), None, None, None),
            P(None, ("half", "bf"), None, None, None),
            P(None, ("half", "bf"), None, None),
            P(None, ("half", "bf")),
        ),
        out_specs=P(None, None, ("half", "bf")),
        check_vma=False,
    )
```

time: 72.1 us -> 37.7 us (0.52)
  starting transfers between devices: 30.5 us -> 0 us
  Pallas kernels: 0 us -> 23.8 us
  local copies, waits for them, and re-layouts: 24.6 us -> 13.4 us
  matrix products: 10.4 us -> 0 us
  other arithmetic: 5.14 us -> 0 us
    all_to_all x2 -> x0, starting transfers between devices: 26.2 us -> none  [the longest x1 13.8 us: local(): lax.all_to_all(fine_flat, 'bf', split_axis=0, concat_axis=0, tiled=True)]
    pallas_call x0 -> x1, Pallas kernels: none -> 23.8 us  [local(): pl.pallas_call(kernel, out_shape=jax.ShapeDtypeStruct(shapes[0], F32), in...]
    dot_general x32 -> x0, matrix products: 10.4 us -> none  [the longest x8 3.2 us: complex_product(): contract(left_imag, right_imag)]
    unnamed x32 -> x21, local copies, waits for them, and re-layouts: 3.54 us -> 13.4 us
    slice x19 -> x0, local copies, waits for them, and re-layouts: 6.5 us -> none  [the longest x17 6.42 us: halves(): return (array[0], array[1])]
    squeeze x12 -> x0, local copies, waits for them, and re-layouts: 6.35 us -> none  [halves(): return (array[0], array[1])]
    ppermute x1 -> x0, starting transfers between devices: 4.3 us -> none  [partner(): return lax.ppermute(block, axis, route)]
    convert_element_type x6 -> x0, other arithmetic: 3.45 us -> none  [the longest x1 1.37 us: local(): sources.astype(jnp.bfloat16).reshape(2, vectors, leaf_count, leaf_len)]
  transfers between devices with their start and end apart: 3 -> 0, of which waited for: 1 -> 0; matrix products, arithmetic and copies ran while one was open for 31% -> 0% of each run, Pallas kernels for 0% -> 0%
where the time goes in v1:
time: 37.7 us; the launch traced here: 37.2 us
  Pallas kernels  23.8 us (63%)
  local copies, waits for them, and re-layouts  13.4 us (36%)
    pallas_call x1, Pallas kernels, local(): pl.pallas_call(kernel, out_shape=jax.ShapeDtypeStruct(shapes[0], F32), in...  23.8 us
    unnamed x21, local copies, waits for them, and re-layouts  13.4 us

profile of v1, /device:TPU:1, one launch (start us, length us, event | category | flops | bytes accessed | tf_op | source)
XLA Modules:
  0.0 37.2 jit_solution(15919533847097496915)
XLA Ops:
  0.0 0.0 copy-start
  0.0 1.6 %copy-done = bf16[2,1,1024,512]{3,2,1,0:T(8,128)(2,1)S(1)} copy-done((bf16[2,1,1024,512]{3,2,1,0:T(8,128)(2,1)S(1)}, bf16[2,1,1024,512]{3,2,1,0:T(8,128)(2,1)}, u32[]{:S(2)}) %copy-start) | copy-done | bytes 2097176
  1.6 0.0 copy-start.1
  1.6 1.6 %copy-done.1 = bf16[2,1,512,1024]{3,2,1,0:T(8,128)(2,1)S(1)} copy-done((bf16[2,1,512,1024]{3,2,1,0:T(8,128)(2,1)S(1)}, bf16[2,1,512,1024]{3,2,1,0:T(8,128)(2,1)}, u32[]{:S(2)}) %copy-start.1) | copy-done | bytes 2097176
  3.2 0.0 copy-start.2
  3.2 1.2 %copy-done.2 = f32[2,32,4096]{2,1,0:T(8,128)S(1)} copy-done((f32[2,32,4096]{2,1,0:T(8,128)S(1)}, f32[2,32,4096]{2,1,0:T(8,128)}, u32[]{:S(2)}) %copy-start.2) | copy-done | bytes 1048600
  4.4 0.0 copy-start.3
  4.4 1.2 %copy-done.3 = bf16[2,16,64,256]{3,2,1,0:T(8,128)(2,1)S(1)} copy-done((bf16[2,16,64,256]{3,2,1,0:T(8,128)(2,1)S(1)}, bf16[2,16,64,256]{3,2,1,0:T(8,128)(2,1)}, u32[]{:S(2)}) %copy-start.3) | copy-done | bytes 1048600
  5.6 0.0 copy-start.4
  5.6 1.2 %copy-done.4 = bf16[2,16,64,256]{3,2,1,0:T(8,128)(2,1)S(1)} copy-done((bf16[2,16,64,256]{3,2,1,0:T(8,128)(2,1)S(1)}, bf16[2,16,64,256]{3,2,1,0:T(8,128)(2,1)}, u32[]{:S(2)}) %copy-start.4) | copy-done | bytes 1048600
  6.9 0.0 copy-start.5
  6.9 1.2 %copy-done.5 = bf16[2,16,64,256]{3,2,1,0:T(8,128)(2,1)S(1)} copy-done((bf16[2,16,64,256]{3,2,1,0:T(8,128)(2,1)S(1)}, bf16[2,16,64,256]{3,2,1,0:T(8,128)(2,1)}, u32[]{:S(2)}) %copy-start.5) | copy-done | bytes 1048600
  8.1 0.0 copy-start.6
  8.1 1.2 %copy-done.6 = bf16[2,1,2,512,256]{4,3,2,1,0:T(8,128)(2,1)S(1)} copy-done((bf16[2,1,2,512,256]{4,3,2,1,0:T(8,128)(2,1)S(1)}, bf16[2,1,2,512,256]{4,3,2,1,0:T(8,128)(2,1)}, u32[]{:S(2)}) %copy-start.6) | copy-done | bytes 1048600
  9.3 0.0 copy-start.7
  9.3 1.2 %copy-done.7 = bf16[2,1,2,256,512]{4,3,2,1,0:T(8,128)(2,1)S(1)} copy-done((bf16[2,1,2,256,512]{4,3,2,1,0:T(8,128)(2,1)S(1)}, bf16[2,1,2,256,512]{4,3,2,1,0:T(8,128)(2,1)}, u32[]{:S(2)}) %copy-start.7) | copy-done | bytes 1048600
  10.5 0.0 copy-start.8
  10.5 1.2 %copy-done.8 = bf16[2,16,64,256]{3,2,1,0:T(8,128)(2,1)S(1)} copy-done((bf16[2,16,64,256]{3,2,1,0:T(8,128)(2,1)S(1)}, bf16[2,16,64,256]{3,2,1,0:T(8,128)(2,1)}, u32[]{:S(2)}) %copy-start.8) | copy-done | bytes 1048600
  11.8 0.0 copy-start.9
  11.8 0.7 %copy-done.9 = s32[4,16]{1,0:T(4,128)S(1)} copy-done((s32[4,16]{1,0:T(4,128)S(1)}, s32[4,16]{1,0:T(4,128)}, u32[]{:S(2)}) %copy-start.9) | copy-done | bytes 280
  12.4 23.8 %shard_map.100 = f32[2,32,4096]{2,1,0:T(8,128)S(1)} custom-call(f32[2,32,4096]{2,1,0:T(8,128)S(1)} %copy-done.2, bf16[2,16,64,256]{3,2,1,0:T(8,128)(2,1)S(1)} %copy-done.3, bf16[2,1,1024,512]{3,2,1,0:T(8,128)(2,1)S(1)} %copy-done, bf16[2,1,512,1024]{3,2,1,0:T(8,128)(2,1)S(1)} %copy-done.1, bf16[2,16,64,256]{3,2,1,0:T(8,128)(2,1)S(1)} %copy-done.4, ...), custom_call_target="tpu_custom_call" | custom-call | flops 672000000 | bytes 12582912 | tf_op jit(solution)/shard_map/pallas_call | solution.py:244
  36.2 1.0 %copy.12 = f32[2,32,4096]{2,1,0:T(8,128)} copy(f32[2,32,4096]{2,1,0:T(8,128)S(1)} %shard_map.100) | data formatting | bytes 2097152
Async XLA Ops:
  0.0 1.6 %copy-start = (bf16[2,1,1024,512]{3,2,1,0:T(8,128)(2,1)S(1)}, bf16[2,1,1024,512]{3,2,1,0:T(8,128)(2,1)}, u32[]{:S(2)}) copy-start(bf16[2,1,1024,512]{3,2,1,0:T(8,128)(2,1)} %coarse_mix_in.1) | copy-start | bytes 6291460
  1.6 1.6 %copy-start.1 = (bf16[2,1,512,1024]{3,2,1,0:T(8,128)(2,1)S(1)}, bf16[2,1,512,1024]{3,2,1,0:T(8,128)(2,1)}, u32[]{:S(2)}) copy-start(bf16[2,1,512,1024]{3,2,1,0:T(8,128)(2,1)} %coarse_mix_out.1) | copy-start | bytes 6291460
  3.2 1.2 %copy-start.2 = (f32[2,32,4096]{2,1,0:T(8,128)S(1)}, f32[2,32,4096]{2,1,0:T(8,128)}, u32[]{:S(2)}) copy-start(f32[2,32,4096]{2,1,0:T(8,128)} %sources.1) | copy-start | bytes 3145732
  4.4 1.2 %copy-start.3 = (bf16[2,16,64,256]{3,2,1,0:T(8,128)(2,1)S(1)}, bf16[2,16,64,256]{3,2,1,0:T(8,128)(2,1)}, u32[]{:S(2)}) copy-start(bf16[2,16,64,256]{3,2,1,0:T(8,128)(2,1)} %coarse_in.1) | copy-start | bytes 3145732
  5.6 1.2 %copy-start.4 = (bf16[2,16,64,256]{3,2,1,0:T(8,128)(2,1)S(1)}, bf16[2,16,64,256]{3,2,1,0:T(8,128)(2,1)}, u32[]{:S(2)}) copy-start(bf16[2,16,64,256]{3,2,1,0:T(8,128)(2,1)} %coarse_out.1) | copy-start | bytes 3145732
  6.9 1.2 %copy-start.5 = (bf16[2,16,64,256]{3,2,1,0:T(8,128)(2,1)S(1)}, bf16[2,16,64,256]{3,2,1,0:T(8,128)(2,1)}, u32[]{:S(2)}) copy-start(bf16[2,16,64,256]{3,2,1,0:T(8,128)(2,1)} %fine_in.1) | copy-start | bytes 3145732
  8.1 1.2 %copy-start.6 = (bf16[2,1,2,512,256]{4,3,2,1,0:T(8,128)(2,1)S(1)}, bf16[2,1,2,512,256]{4,3,2,1,0:T(8,128)(2,1)}, u32[]{:S(2)}) copy-start(bf16[2,1,2,512,256]{4,3,2,1,0:T(8,128)(2,1)} %fine_mix_in.1) | copy-start | bytes 3145732
  9.3 1.2 %copy-start.7 = (bf16[2,1,2,256,512]{4,3,2,1,0:T(8,128)(2,1)S(1)}, bf16[2,1,2,256,512]{4,3,2,1,0:T(8,128)(2,1)}, u32[]{:S(2)}) copy-start(bf16[2,1,2,256,512]{4,3,2,1,0:T(8,128)(2,1)} %fine_mix_out.1) | copy-start | bytes 3145732
  10.5 1.2 %copy-start.8 = (bf16[2,16,64,256]{3,2,1,0:T(8,128)(2,1)S(1)}, bf16[2,16,64,256]{3,2,1,0:T(8,128)(2,1)}, u32[]{:S(2)}) copy-start(bf16[2,16,64,256]{3,2,1,0:T(8,128)(2,1)} %fine_out.1) | copy-start | bytes 3145732
  11.8 0.7 %copy-start.9 = (s32[4,16]{1,0:T(4,128)S(1)}, s32[4,16]{1,0:T(4,128)}, u32[]{:S(2)}) copy-start(s32[4,16]{1,0:T(4,128)} %ranks.1) | copy-start | bytes 772

commit v2 on v1

--- a/solution.py
+++ b/solution.py
@@ -43,8 +43,8 @@
     out,
     x_v, ci_v, cmi_v, cmo_v, co_v, fi_v, fmi_v, fmo_v, fo_v, ranks_s,
     regroup, pairs, spread, ccoef, fcoef, cback, fback,
-    cs1, cr1, cs2, cr2, fs1, fr1, fs2, fr2, out_v,
-    in_sem, send_sem, recv_sem, out_sem,
+    cs1, cr1, cs2, cr2, fs1, fr1, fs2, fr2,
+    in_sem, send_sem, recv_sem,
 ):
     half = lax.axis_index("half")
     block = lax.axis_index("bf")
@@ -223,29 +223,23 @@
                 [jnp.concatenate([re, -im], axis=1), jnp.concatenate([im, re], axis=1)], axis=0
             ).astype(BF16)
             w = jnp.concatenate([two[0][0, s], two[1][0, s], two[0][1, s], two[1][1, s]], axis=0)
-            out_v[:, :, s * LEAF : (s + 1) * LEAF] = dot(left, w).reshape(2, VECTORS, LEAF)
-        if first % per == per - 2:
-            span = pl.ds((first + 2 - per) * LEAF, per * LEAF)
-            pltpu.make_async_copy(out_v.at[:, :, span], out.at[:, :, span], out_sem.at[first // per]).start()
+            out[:, :, s * LEAF : (s + 1) * LEAF] = dot(left, w).reshape(2, VECTORS, LEAF)
 
     sent(cs1, 0)
     sent(fs1.at[pl.ds(0, GROUPS - 1)], 1)
     sent(cs2.at[pl.ds(0, MEMBERS - 1)], 2)
     sent(fs2.at[pl.ds(0, MEMBERS - 1)], 3)
-    for c in range(CHUNKS):
-        span = pl.ds(c * per * LEAF, per * LEAF)
-        pltpu.make_async_copy(out_v.at[:, :, span], out.at[:, :, span], out_sem.at[c]).wait()
 
 
 def local(*args):
-    anywhere = pl.BlockSpec(memory_space=pl.ANY)
+    hbm = pl.BlockSpec(memory_space=pltpu.HBM)
     shapes = [a.shape for a in args]
     vmem = pltpu.VMEM
     return pl.pallas_call(
         kernel,
         out_shape=jax.ShapeDtypeStruct(shapes[0], F32),
-        in_specs=[anywhere] * len(args),
-        out_specs=anywhere,
+        in_specs=[hbm] * len(args),
+        out_specs=pl.BlockSpec(memory_space=pltpu.VMEM),
         scratch_shapes=[
             vmem(shapes[0], F32),
             *[vmem(s, BF16) for s in shapes[1:9]],
@@ -264,17 +258,15 @@
                 ]
                 * 2
             ],
-            vmem(shapes[0], F32),
             pltpu.SemaphoreType.DMA((1 + 3 * CHUNKS + 6,)),
             pltpu.SemaphoreType.DMA((4,)),
             pltpu.SemaphoreType.DMA((4,)),
-            pltpu.SemaphoreType.DMA((CHUNKS,)),
         ],
         compiler_params=pltpu.CompilerParams(
             collective_id=0, has_side_effects=True, vmem_limit_bytes=40 * 1024 * 1024
         ),
         cost_estimate=pl.CostEstimate(flops=672 * 10**6, bytes_accessed=12 * 2**20, transcendentals=0),
-    )(*args)
+    )(*[pltpu.with_memory_space_constraint(a, pltpu.HBM) for a in args])
 
 
 def solution(mesh):

time: 37.7 us -> 24.9 us (0.66)
  local copies, waits for them, and re-layouts: 13.4 us -> 0.97 us
    unnamed x21 -> x1, local copies, waits for them, and re-layouts: 13.4 us -> 0.97 us
where the time goes in v2:
time: 24.9 us; the launch traced here: 24.8 us
  Pallas kernels  23.8 us (96%)
  local copies, waits for them, and re-layouts  0.97 us (4%)
    pallas_call x1, Pallas kernels, local(): pl.pallas_call(kernel, out_shape=jax.ShapeDtypeStruct(shapes[0], F32), in...  23.8 us
    unnamed x1, local copies, waits for them, and re-layouts  0.97 us

profile of v2, /device:TPU:1, one launch (start us, length us, event | category | flops | bytes accessed | tf_op | source)
XLA Modules:
  0.0 24.8 jit_solution(16299398272727505769)
XLA Ops:
  0.0 23.8 %shard_map.100 = f32[2,32,4096]{2,1,0:T(8,128)S(1)} custom-call(f32[2,32,4096]{2,1,0:T(8,128)} %sources.1, bf16[2,16,64,256]{3,2,1,0:T(8,128)(2,1)} %coarse_in.1, bf16[2,1,1024,512]{3,2,1,0:T(8,128)(2,1)} %coarse_mix_in.1, bf16[2,1,512,1024]{3,2,1,0:T(8,128)(2,1)} %coarse_mix_out.1, bf16[2,16,64,256]{3,2,1,0:T(8,128)(2,1)} %coarse_out.1, ...), custom_call_target="tpu_custom_call" | custom-call | flops 672000000 | bytes 12582912 | tf_op jit(solution)/shard_map/pallas_call | solution.py:238
  23.8 1.0 %copy.12 = f32[2,32,4096]{2,1,0:T(8,128)} copy(f32[2,32,4096]{2,1,0:T(8,128)S(1)} %shard_map.100) | data formatting | bytes 2097152

commit v3 on v2

--- a/solution.py
+++ b/solution.py
@@ -10,14 +10,14 @@
 F32 = jnp.float32
 BF16 = jnp.bfloat16
 MESH = pl.DeviceIdType.MESH
-GROUPS = 8
-MEMBERS = 16
-ROWS = 32
+CORES = 2
+CHIPS = 64
+RING = 4
 LEAVES = 16
 RANK = 64
 LEAF = 256
 VECTORS = 32
-CHUNKS = 4
+CHUNKS = 2
 
 
 def dot(left, right):
@@ -30,6 +30,13 @@
 
 def iota(shape, axis):
     return lax.broadcasted_iota(jnp.int32, shape, axis)
+
+
+def farthest_first(apart):
+    ways = [(0, 1.5, 2, 1.5), (4, 2.5, 2, 2.5)][apart]
+    ring = (0, 1, 2, 1)
+    steps = [(z, y, x) for z in range(RING) for y in range(RING) for x in range(RING)]
+    return sorted(steps, key=lambda s: -(ways[s[0]] + ring[s[1]] + ring[s[2]]))
 
 
 def complex_rows(by_real, by_imag):
@@ -42,14 +49,26 @@
     fine_in, fine_mix_in, fine_mix_out, fine_out, ranks,
     out,
     x_v, ci_v, cmi_v, cmo_v, co_v, fi_v, fmi_v, fmo_v, fo_v, ranks_s,
-    regroup, pairs, spread, ccoef, fcoef, cback, fback,
-    cs1, cr1, cs2, cr2, fs1, fr1, fs2, fr2,
+    square, wide, ccoef, fcoef, cback, fback,
+    c_put, c_got, c_core, f_put, f_got, f_core,
     in_sem, send_sem, recv_sem,
 ):
     half = lax.axis_index("half")
     block = lax.axis_index("bf")
-    group = block // MEMBERS
-    member = block % MEMBERS
+    core = block % CORES
+    chip = block // CORES
+    at_z, at_y, at_x = chip // (RING * RING), chip // RING % RING, chip % RING
+    zs = [(at_z + k) % RING * (RING * RING) for k in range(RING)]
+    ys = [(at_y + k) % RING * RING for k in range(RING)]
+    xs = [(at_x + k) % RING for k in range(RING)]
+
+    def chips(apart):
+        return [zs[z] + ys[y] + xs[x] for z, y, x in farthest_first(apart) if apart or z + y + x]
+
+    barrier = pltpu.get_barrier_semaphore()
+
+    def greet(h, b):
+        pl.semaphore_signal(barrier, inc=1, device_id=(h, b), device_id_type=MESH)
 
     per = LEAVES // CHUNKS
     loads = {}
@@ -68,33 +87,21 @@
         load(("fi", c), fine_in.at[:, span], fi_v.at[:, span])
     load("cmi", coarse_mix_in, cmi_v)
     load("fmi", fine_mix_in, fmi_v)
+    for there in chips(1):
+        greet(1 - half, there * CORES + core)
+    for there in chips(0):
+        greet(half, there * CORES + core)
+    greet(half, chip * CORES + 1 - core)
+    load("fmo", fine_mix_out, fmo_v)
     load("cmo", coarse_mix_out, cmo_v)
-    load("fmo", fine_mix_out, fmo_v)
     load("co", coarse_out, co_v)
     load("fo", fine_out, fo_v)
 
-    barrier = pltpu.get_barrier_semaphore()
-
-    def greet(h, b):
-        pl.semaphore_signal(barrier, inc=1, device_id=(h, b), device_id_type=MESH)
-
-    for k in range(GROUPS):
-        there = (group + k) % GROUPS * MEMBERS + member
-        greet(1 - half, there)
-        if k:
-            greet(half, there)
-    for k in range(1, MEMBERS):
-        greet(half, group * MEMBERS + (member + k) % MEMBERS)
-
-    def regrouped(row):
-        return row // 2 % GROUPS * ROWS + row // (2 * GROUPS) * 2 + row % 2
-
-    rows = iota((256, 256), 0)
-    regroup[...] = (regrouped(rows) == iota((256, 256), 1)).astype(F32).astype(BF16)
-    rows = iota((256, 512), 0)
-    cols = iota((256, 512), 1) // 2
-    spread[...] = (regrouped(rows) == cols).astype(F32).astype(BF16)
-    pairs[...] = (rows == cols).astype(F32).astype(BF16)
+    def taken(row):
+        return row % 128 // 2 * 4 + (core + row // 128) % 2 * 2 + row % 2
+
+    square[...] = (taken(iota((256, 256), 0)) == iota((256, 256), 1)).astype(F32).astype(BF16)
+    wide[...] = (taken(iota((256, 512), 0)) == iota((256, 512), 1) // 2).astype(F32).astype(BF16)
 
     lane = iota((1, 128), 1)
     low = lane < RANK
@@ -139,12 +146,16 @@
     send = jnp.concatenate([re, im], axis=0)
     even = iota((1, 512), 1) % 2 == 0
     send = jnp.concatenate([jnp.where(even, send, 0.0), jnp.where(even, 0.0, send)], axis=0).astype(BF16)
-    cs1[...] = dot_t(pairs[...], send).astype(BF16).reshape(GROUPS, ROWS, 128)
-
-    pl.semaphore_wait(barrier, 2 * GROUPS - 1 + MEMBERS - 1)
-    for k in range(GROUPS):
-        there = (group + k) % GROUPS
-        remote(cs1.at[there], cr1.at[group], 0, 1 - half, there * MEMBERS + member)
+    c_put[...] = dot_t(wide[...], send).astype(BF16).reshape(c_put.shape)
+
+    def send_coarse():
+        for there in chips(1):
+            remote(c_put.at[:, there], c_got.at[:, chip], 0, 1 - half, there * CORES + core)
+
+    @pl.when(half == 1)
+    def _():
+        pl.semaphore_wait(barrier, 2 * CHIPS)
+        send_coarse()
 
     loads["fmi"].wait()
     fine = []
@@ -159,39 +170,26 @@
             parts.append(dot(left, w))
         fine.extend(complex_rows(*parts))
     send = jnp.concatenate(fine, axis=0)
-    fs1[...] = send.T.astype(BF16).reshape(GROUPS, ROWS, 128)
-    for k in range(1, GROUPS):
-        there = (group + k) % GROUPS
-        remote(fs1.at[there], fr1.at[group], 1, half, there * MEMBERS + member)
-    pltpu.make_async_copy(fs1.at[group], fr1.at[group], recv_sem.at[1]).start()
-
-    def pass_on(received, outgoing, landing, first, which):
-        arrived(received, first)
-        rows = received[...].reshape(256, 128)
-        outgoing[...] = dot(regroup[...], rows).astype(BF16).reshape(MEMBERS, 2 * GROUPS, 128)
-        for k in range(1, MEMBERS):
-            there = (member + k) % MEMBERS
-            remote(outgoing.at[there], landing.at[member], which, half, group * MEMBERS + there)
-        pltpu.make_async_copy(outgoing.at[member], landing.at[member], recv_sem.at[which]).start()
-
-    pass_on(cr1, cs2, cr2, 0, 2)
-    pass_on(fr1, fs2, fr2, 1, 3)
-
-    arrived(cr2, 2)
-    got = dot(cr2[...].reshape(256, 128).T, spread[...])
-    left = jnp.where(even, got[:64], got[64:]).astype(BF16)
-    loads["cmo"].wait()
-    for at in range(0, 1024, 256):
-        re, im = complex_rows(dot(left, cmo_v[0, 0, :, at : at + 256]), dot(left, cmo_v[1, 0, :, at : at + 256]))
-        for n in range(2):
-            leaf = at // RANK + 2 * n
-            kept = keep(ranks_s[1, leaf], ranks_s[1, leaf + 1])
-            cols = slice(128 * n, 128 * n + 128)
-            cback[0, :, at + 128 * n : at + 128 * n + 128] = jnp.where(kept, re[:, cols], 0.0)
-            cback[1, :, at + 128 * n : at + 128 * n + 128] = jnp.where(kept, im[:, cols], 0.0)
-
-    arrived(fr2, 3)
-    got = dot(fr2[...].reshape(256, 128).T, regroup[...]).astype(BF16)
+    f_put[...] = dot_t(square[...], send.astype(BF16)).astype(BF16).reshape(f_put.shape)
+    @pl.when(half == 0)
+    def _():
+        pl.semaphore_wait(barrier, 2 * CHIPS)
+
+    for there in chips(0):
+        remote(f_put.at[:, there], f_got.at[:, chip], 1, half, there * CORES + core)
+    pltpu.make_async_copy(f_put.at[:, chip], f_got.at[:, chip], recv_sem.at[1]).start()
+
+    @pl.when(half == 0)
+    def _():
+        send_coarse()
+
+    def rows_of(got, landing, which):
+        arrived(landing, which)
+        return jnp.concatenate([got[0].reshape(128, 128), landing[...].reshape(128, 128)], axis=0)
+
+    arrived(f_got, 1)
+    remote(f_got.at[1], f_core, 3, half, chip * CORES + 1 - core)
+    got = dot(rows_of(f_got, f_core, 3).T, square[...]).astype(BF16)
     loads["fmo"].wait()
     for i in range(2):
         left = got[i * 64 : i * 64 + 64]
@@ -206,6 +204,20 @@
                 cols = slice(128 * n, 128 * n + 128)
                 fback[0, :, place : place + 128] = pltpu.roll(jnp.where(kept, re[:, cols], 0.0), RANK, 1)
                 fback[1, :, place : place + 128] = pltpu.roll(jnp.where(kept, im[:, cols], 0.0), RANK, 1)
+
+    arrived(c_got, 0)
+    remote(c_got.at[1], c_core, 2, half, chip * CORES + 1 - core)
+    got = dot(rows_of(c_got, c_core, 2).T, wide[...])
+    left = jnp.where(even, got[:64], got[64:]).astype(BF16)
+    loads["cmo"].wait()
+    for at in range(0, 1024, 256):
+        re, im = complex_rows(dot(left, cmo_v[0, 0, :, at : at + 256]), dot(left, cmo_v[1, 0, :, at : at + 256]))
+        for n in range(2):
+            leaf = at // RANK + 2 * n
+            kept = keep(ranks_s[1, leaf], ranks_s[1, leaf + 1])
+            cols = slice(128 * n, 128 * n + 128)
+            cback[0, :, at + 128 * n : at + 128 * n + 128] = jnp.where(kept, re[:, cols], 0.0)
+            cback[1, :, at + 128 * n : at + 128 * n + 128] = jnp.where(kept, im[:, cols], 0.0)
 
     loads["co"].wait()
     loads["fo"].wait()
@@ -225,10 +237,10 @@
             w = jnp.concatenate([two[0][0, s], two[1][0, s], two[0][1, s], two[1][1, s]], axis=0)
             out[:, :, s * LEAF : (s + 1) * LEAF] = dot(left, w).reshape(2, VECTORS, LEAF)
 
-    sent(cs1, 0)
-    sent(fs1.at[pl.ds(0, GROUPS - 1)], 1)
-    sent(cs2.at[pl.ds(0, MEMBERS - 1)], 2)
-    sent(fs2.at[pl.ds(0, MEMBERS - 1)], 3)
+    sent(c_put, 0)
+    sent(f_put.at[:, pl.ds(0, CHIPS - 1)], 1)
+    sent(c_core, 2)
+    sent(f_core, 3)
 
 
 def local(*args):
@@ -246,18 +258,11 @@
             pltpu.SMEM(shapes[9], jnp.int32),
             vmem((256, 256), BF16),
             vmem((256, 512), BF16),
-            vmem((256, 512), BF16),
             vmem((64, 1024), BF16),
             vmem((64, 1024), BF16),
             vmem((2, 32, 1024), F32),
             vmem((2, 32, 1024), F32),
-            *[
-                vmem(s, BF16)
-                for s in [
-                    (GROUPS, ROWS, 128), (GROUPS, ROWS, 128), (MEMBERS, 2 * GROUPS, 128), (MEMBERS, 2 * GROUPS, 128),
-                ]
-                * 2
-            ],
+            *[vmem(s, BF16) for s in [(CORES, CHIPS, 2, 128), (CORES, CHIPS, 2, 128), (CHIPS, 2, 128)] * 2],
             pltpu.SemaphoreType.DMA((1 + 3 * CHUNKS + 6,)),
             pltpu.SemaphoreType.DMA((4,)),
             pltpu.SemaphoreType.DMA((4,)),

time: 24.9 us -> 22.5 us (0.904)
  Pallas kernels: 23.8 us -> 21.4 us
    pallas_call x1, Pallas kernels: 23.8 us -> 21.4 us  [local(): pl.pallas_call(kernel, out_shape=jax.ShapeDtypeStruct(shapes[0], F32), in...]
where the time goes in v3:
time: 22.5 us; the launch traced here: 22.4 us
  Pallas kernels  21.4 us (95%)
  local copies, waits for them, and re-layouts  0.97 us (4%)
    pallas_call x1, Pallas kernels, local(): pl.pallas_call(kernel, out_shape=jax.ShapeDtypeStruct(shapes[0], F32), in...  21.4 us
    unnamed x1, local copies, waits for them, and re-layouts  0.97 us

profile of v3, /device:TPU:1, one launch (start us, length us, event | category | flops | bytes accessed | tf_op | source)
XLA Modules:
  0.0 22.4 jit_solution(7028427914740824758)
XLA Ops:
  0.0 21.4 %shard_map.100 = f32[2,32,4096]{2,1,0:T(8,128)S(1)} custom-call(f32[2,32,4096]{2,1,0:T(8,128)} %sources.1, bf16[2,16,64,256]{3,2,1,0:T(8,128)(2,1)} %coarse_in.1, bf16[2,1,1024,512]{3,2,1,0:T(8,128)(2,1)} %coarse_mix_in.1, bf16[2,1,512,1024]{3,2,1,0:T(8,128)(2,1)} %coarse_mix_out.1, bf16[2,16,64,256]{3,2,1,0:T(8,128)(2,1)} %coarse_out.1, ...), custom_call_target="tpu_custom_call" | custom-call | flops 672000000 | bytes 12582912 | tf_op jit(solution)/shard_map/pallas_call | solution.py:250
  21.5 1.0 %copy.12 = f32[2,32,4096]{2,1,0:T(8,128)} copy(f32[2,32,4096]{2,1,0:T(8,128)S(1)} %shard_map.100) | data formatting | bytes 2097152

commit v4 on v3

--- a/solution.py
+++ b/solution.py
@@ -18,6 +18,7 @@
 LEAF = 256
 VECTORS = 32
 CHUNKS = 2
+MIX_CHUNKS = 4
 
 
 def dot(left, right):
@@ -49,9 +50,9 @@
     fine_in, fine_mix_in, fine_mix_out, fine_out, ranks,
     out,
     x_v, ci_v, cmi_v, cmo_v, co_v, fi_v, fmi_v, fmo_v, fo_v, ranks_s,
-    square, wide, ccoef, fcoef, cback, fback,
+    square, wide, ccoef, fcoef, fback,
     c_put, c_got, c_core, f_put, f_got, f_core,
-    in_sem, send_sem, recv_sem,
+    in_sem, send_sem, recv_sem, coarse_ok, fine_ok,
 ):
     half = lax.axis_index("half")
     block = lax.axis_index("bf")
@@ -71,6 +72,7 @@
         pl.semaphore_signal(barrier, inc=1, device_id=(h, b), device_id_type=MESH)
 
     per = LEAVES // CHUNKS
+    deep = LEAVES * RANK // MIX_CHUNKS
     loads = {}
 
     def load(name, source, target):
@@ -84,14 +86,25 @@
         cols = pl.ds(c * per * LEAF, per * LEAF)
         load(("x", c), sources.at[:, :, cols], x_v.at[:, :, cols])
         load(("ci", c), coarse_in.at[:, span], ci_v.at[:, span])
-        load(("fi", c), fine_in.at[:, span], fi_v.at[:, span])
-    load("cmi", coarse_mix_in, cmi_v)
+    for c in range(MIX_CHUNKS):
+        span = pl.ds(c * deep, deep)
+        load(("cmi", c), coarse_mix_in.at[:, :, span], cmi_v.at[:, :, span])
+    load("fi", fine_in, fi_v)
     load("fmi", fine_mix_in, fmi_v)
+    greet(half, chip * CORES + 1 - core)
     for there in chips(1):
-        greet(1 - half, there * CORES + core)
+        greet(1 - half, there * CORES + 1)
     for there in chips(0):
-        greet(half, there * CORES + core)
-    greet(half, chip * CORES + 1 - core)
+        greet(half, there * CORES)
+
+    def tell(semaphore):
+        to = (half, chip * CORES + 1 - core)
+        pl.semaphore_signal(semaphore, inc=1, device_id=to, device_id_type=MESH)
+
+    def hear_other_half():
+        pl.semaphore_wait(barrier, CORES * CHIPS + 1)
+        tell(coarse_ok)
+
     load("fmo", fine_mix_out, fmo_v)
     load("cmo", coarse_mix_out, cmo_v)
     load("co", coarse_out, co_v)
@@ -109,29 +122,31 @@
     def keep(first, second):
         return lane < jnp.where(low, first, second + RANK)
 
+    def swapped(two):
+        return pltpu.roll(two, RANK, 1)
+
+    def column_pair(factor, which, first):
+        mixed = []
+        for s in (first, first + 1):
+            x = x_v[:, :, s * LEAF : (s + 1) * LEAF].astype(BF16).reshape(2 * VECTORS, LEAF)
+            order = (0, 1) if s == first else (1, 0)
+            y = dot_t(x, jnp.concatenate([factor[order[0], s], factor[order[1], s]], axis=0))
+            mine, other = y[:VECTORS], swapped(y[VECTORS:])
+            mixed.append(mine + jnp.where(low == (s == first), -other, other))
+        both = [jnp.where(low, mixed[0], mixed[1]), swapped(jnp.where(low, mixed[1], mixed[0]))]
+        kept = keep(ranks_s[which, first], ranks_s[which, first + 1])
+        return jnp.where(kept, jnp.concatenate(both, axis=0), 0.0).astype(BF16)
+
     loads["ranks"].wait()
     for c in range(CHUNKS):
-        for name in ("x", "ci", "fi"):
-            loads[name, c].wait()
+        loads["x", c].wait()
+        loads["ci", c].wait()
         for first in range(c * per, (c + 1) * per, 2):
-            got = []
-            for s in (first, first + 1):
-                x = x_v[:, :, s * LEAF : (s + 1) * LEAF].astype(BF16).reshape(2 * VECTORS, LEAF)
-                two = (ci_v, fi_v) if s == first else (fi_v, ci_v)
-                w = jnp.concatenate([two[0][0, s], two[1][0, s], two[0][1, s], two[1][1, s]], axis=0)
-                y = dot_t(x, w)
-                re, im = complex_rows(y[:, :128], y[:, 128:])
-                which = (0, 2) if s == first else (2, 0)
-                kept = keep(ranks_s[which[0], s], ranks_s[which[1], s])
-                both = jnp.concatenate([re, im], axis=0)
-                got.append(jnp.where(kept, both, 0.0))
-            at = pl.ds(first * RANK, 2 * RANK)
-            ccoef[:, at] = jnp.where(low, got[0], got[1]).astype(BF16)
-            fcoef[:, at] = jnp.where(low, got[1], got[0]).astype(BF16)
-
-    def remote(source, target, which, h, b):
+            ccoef[:, first * RANK : (first + 2) * RANK] = column_pair(ci_v, 0, first)
+
+    def remote(source, target, which, h, b, out=None):
         pltpu.make_async_remote_copy(
-            src_ref=source, dst_ref=target, send_sem=send_sem.at[which], recv_sem=recv_sem.at[which],
+            src_ref=source, dst_ref=target, send_sem=send_sem.at[which if out is None else out], recv_sem=recv_sem.at[which],
             device_id=(h, b), device_id_type=MESH,
         ).start()
 
@@ -141,47 +156,72 @@
     def sent(buffer, which):
         pltpu.make_async_copy(buffer, buffer, send_sem.at[which]).wait()
 
-    loads["cmi"].wait()
-    re, im = complex_rows(dot(ccoef[...], cmi_v[0, 0]), dot(ccoef[...], cmi_v[1, 0]))
+    @pl.when((half == 1) & (core == 1))
+    def _():
+        hear_other_half()
+
+    sums = [0.0, 0.0]
+    for c in range(MIX_CHUNKS):
+        loads["cmi", c].wait()
+        span = slice(c * deep, (c + 1) * deep)
+        sums = [sums[part] + dot(ccoef[:, span], cmi_v[part, 0, span]) for part in range(2)]
+    re, im = complex_rows(*sums)
     send = jnp.concatenate([re, im], axis=0)
     even = iota((1, 512), 1) % 2 == 0
     send = jnp.concatenate([jnp.where(even, send, 0.0), jnp.where(even, 0.0, send)], axis=0).astype(BF16)
     c_put[...] = dot_t(wide[...], send).astype(BF16).reshape(c_put.shape)
 
-    def send_coarse():
+    def send_coarse(direct):
         for there in chips(1):
-            remote(c_put.at[:, there], c_got.at[:, chip], 0, 1 - half, there * CORES + core)
+            if direct:
+                for k, target in enumerate((c_got.at[0, chip], c_core.at[chip])):
+                    to = there * CORES + (core + k) % CORES
+                    remote(c_put.at[k, there], target, 2 * k, 0, to)
+            else:
+                remote(c_put.at[:, there], c_got.at[:, chip], 0, 1, there * CORES + core)
+
+    @pl.when((half == 1) & (core == 0))
+    def _():
+        pl.semaphore_wait(coarse_ok, 1)
 
     @pl.when(half == 1)
     def _():
-        pl.semaphore_wait(barrier, 2 * CHIPS)
-        send_coarse()
-
+        send_coarse(True)
+
+    loads["fi"].wait()
+    for first in range(0, LEAVES, 2):
+        fcoef[:, first * RANK : (first + 2) * RANK] = column_pair(fi_v, 2, first)
     loads["fmi"].wait()
     fine = []
     for i in range(2):
         left = fcoef[:, i * 512 : (i + 1) * 512]
-        parts = []
-        for part in range(2):
-            order = [leaf ^ 1 for leaf in range(LEAVES // 2)]
-            w = jnp.concatenate(
-                [fmi_v[part, 0, i, leaf * RANK : (leaf + 1) * RANK, :] for leaf in order], axis=0
-            )
-            parts.append(dot(left, w))
-        fine.extend(complex_rows(*parts))
+        fine.extend(complex_rows(dot(left, fmi_v[0, 0, i]), dot(left, fmi_v[1, 0, i])))
     send = jnp.concatenate(fine, axis=0)
     f_put[...] = dot_t(square[...], send.astype(BF16)).astype(BF16).reshape(f_put.shape)
-    @pl.when(half == 0)
-    def _():
-        pl.semaphore_wait(barrier, 2 * CHIPS)
+    @pl.when(core == 0)
+    def _():
+        pl.semaphore_wait(barrier, CORES * (CHIPS - 1) + 1)
+        tell(fine_ok)
+
+    @pl.when(core == 1)
+    def _():
+        pl.semaphore_wait(fine_ok, 1)
 
     for there in chips(0):
         remote(f_put.at[:, there], f_got.at[:, chip], 1, half, there * CORES + core)
     pltpu.make_async_copy(f_put.at[:, chip], f_got.at[:, chip], recv_sem.at[1]).start()
 
+    @pl.when((half == 0) & (core == 1))
+    def _():
+        hear_other_half()
+
+    @pl.when((half == 0) & (core == 0))
+    def _():
+        pl.semaphore_wait(coarse_ok, 1)
+
     @pl.when(half == 0)
     def _():
-        send_coarse()
+        send_coarse(False)
 
     def rows_of(got, landing, which):
         arrived(landing, which)
@@ -205,41 +245,51 @@
                 fback[0, :, place : place + 128] = pltpu.roll(jnp.where(kept, re[:, cols], 0.0), RANK, 1)
                 fback[1, :, place : place + 128] = pltpu.roll(jnp.where(kept, im[:, cols], 0.0), RANK, 1)
 
-    arrived(c_got, 0)
-    remote(c_got.at[1], c_core, 2, half, chip * CORES + 1 - core)
+    @pl.when(half == 0)
+    def _():
+        arrived(c_got.at[0], 0)
+
+    @pl.when(half == 1)
+    def _():
+        arrived(c_got, 0)
+        remote(c_got.at[1], c_core, 2, 1, chip * CORES + 1 - core, 4)
+
     got = dot(rows_of(c_got, c_core, 2).T, wide[...])
     left = jnp.where(even, got[:64], got[64:]).astype(BF16)
     loads["cmo"].wait()
-    for at in range(0, 1024, 256):
-        re, im = complex_rows(dot(left, cmo_v[0, 0, :, at : at + 256]), dot(left, cmo_v[1, 0, :, at : at + 256]))
-        for n in range(2):
-            leaf = at // RANK + 2 * n
-            kept = keep(ranks_s[1, leaf], ranks_s[1, leaf + 1])
-            cols = slice(128 * n, 128 * n + 128)
-            cback[0, :, at + 128 * n : at + 128 * n + 128] = jnp.where(kept, re[:, cols], 0.0)
-            cback[1, :, at + 128 * n : at + 128 * n + 128] = jnp.where(kept, im[:, cols], 0.0)
-
     loads["co"].wait()
     loads["fo"].wait()
-    for first in range(0, LEAVES, 2):
-        at = slice(first * RANK, first * RANK + 128)
-        cr, ci, fr, fi = cback[0, :, at], cback[1, :, at], fback[0, :, at], fback[1, :, at]
-        for s in (first, first + 1):
-            if s == first:
-                re, im = jnp.where(low, cr, fr), jnp.where(low, ci, fi)
-                two = (co_v, fo_v)
-            else:
-                re, im = jnp.where(low, fr, cr), jnp.where(low, fi, ci)
-                two = (fo_v, co_v)
-            left = jnp.concatenate(
-                [jnp.concatenate([re, -im], axis=1), jnp.concatenate([im, re], axis=1)], axis=0
-            ).astype(BF16)
-            w = jnp.concatenate([two[0][0, s], two[1][0, s], two[0][1, s], two[1][1, s]], axis=0)
-            out[:, :, s * LEAF : (s + 1) * LEAF] = dot(left, w).reshape(2, VECTORS, LEAF)
-
-    sent(c_put, 0)
+    for at in range(0, 1024, 256):
+        pair = complex_rows(dot(left, cmo_v[0, 0, :, at : at + 256]), dot(left, cmo_v[1, 0, :, at : at + 256]))
+        for n in range(2):
+            first = at // RANK + 2 * n
+            kept = keep(ranks_s[1, first], ranks_s[1, first + 1])
+            cr, ci = [jnp.where(kept, part[:, 128 * n : 128 * n + 128], 0.0) for part in pair]
+            cols = slice(first * RANK, first * RANK + 128)
+            fr, fi = fback[0, :, cols], fback[1, :, cols]
+            for s in (first, first + 1):
+                if s == first:
+                    re, im = jnp.where(low, cr, fr), jnp.where(low, ci, fi)
+                    two = (co_v, fo_v)
+                else:
+                    re, im = jnp.where(low, fr, cr), jnp.where(low, fi, ci)
+                    two = (fo_v, co_v)
+                rows = [jnp.concatenate([re, -im], axis=1), jnp.concatenate([im, re], axis=1)]
+                w = jnp.concatenate([two[0][0, s], two[1][0, s], two[0][1, s], two[1][1, s]], axis=0)
+                y = dot(jnp.concatenate(rows, axis=0).astype(BF16), w)
+                out[:, :, s * LEAF : (s + 1) * LEAF] = y.reshape(2, VECTORS, LEAF)
+
+    @pl.when(half == 0)
+    def _():
+        sent(c_put, 0)
+
+    @pl.when(half == 1)
+    def _():
+        sent(c_put.at[0], 0)
+        sent(c_put.at[1], 2)
+        sent(c_core, 4)
+
     sent(f_put.at[:, pl.ds(0, CHIPS - 1)], 1)
-    sent(c_core, 2)
     sent(f_core, 3)
 
 
@@ -261,11 +311,12 @@
             vmem((64, 1024), BF16),
             vmem((64, 1024), BF16),
             vmem((2, 32, 1024), F32),
-            vmem((2, 32, 1024), F32),
             *[vmem(s, BF16) for s in [(CORES, CHIPS, 2, 128), (CORES, CHIPS, 2, 128), (CHIPS, 2, 128)] * 2],
-            pltpu.SemaphoreType.DMA((1 + 3 * CHUNKS + 6,)),
+            pltpu.SemaphoreType.DMA((1 + 2 * CHUNKS + MIX_CHUNKS + 6,)),
+            pltpu.SemaphoreType.DMA((5,)),
             pltpu.SemaphoreType.DMA((4,)),
-            pltpu.SemaphoreType.DMA((4,)),
+            pltpu.SemaphoreType.REGULAR,
+            pltpu.SemaphoreType.REGULAR,
         ],
         compiler_params=pltpu.CompilerParams(
             collective_id=0, has_side_effects=True, vmem_limit_bytes=40 * 1024 * 1024

time: 22.5 us -> 20.8 us (0.924)
  Pallas kernels: 21.4 us -> 19.8 us
    pallas_call x1, Pallas kernels: 21.4 us -> 19.8 us  [local(): pl.pallas_call(kernel, out_shape=jax.ShapeDtypeStruct(shapes[0], F32), in...]
where the time goes in v4:
time: 20.8 us
  Pallas kernels  19.8 us (95%)
  local copies, waits for them, and re-layouts  0.97 us (5%)
    pallas_call x1, Pallas kernels, local(): pl.pallas_call(kernel, out_shape=jax.ShapeDtypeStruct(shapes[0], F32), in...  19.8 us
    unnamed x1, local copies, waits for them, and re-layouts  0.97 us

profile of v4, /device:TPU:1, one launch (start us, length us, event | category | flops | bytes accessed | tf_op | source)
XLA Modules:
  0.0 20.8 jit_solution(10363217594024910932)
XLA Ops:
  0.0 19.8 %shard_map.100 = f32[2,32,4096]{2,1,0:T(8,128)S(1)} custom-call(f32[2,32,4096]{2,1,0:T(8,128)} %sources.1, bf16[2,16,64,256]{3,2,1,0:T(8,128)(2,1)} %coarse_in.1, bf16[2,1,1024,512]{3,2,1,0:T(8,128)(2,1)} %coarse_mix_in.1, bf16[2,1,512,1024]{3,2,1,0:T(8,128)(2,1)} %coarse_mix_out.1, bf16[2,16,64,256]{3,2,1,0:T(8,128)(2,1)} %coarse_out.1, ...), custom_call_target="tpu_custom_call" | custom-call | flops 672000000 | bytes 12582912 | tf_op jit(solution)/shard_map/pallas_call | solution.py:300
  19.8 1.0 %copy.12 = f32[2,32,4096]{2,1,0:T(8,128)} copy(f32[2,32,4096]{2,1,0:T(8,128)S(1)} %shard_map.100) | data formatting | bytes 2097152

commit v5 on v4

--- a/solution.py
+++ b/solution.py
@@ -12,6 +12,7 @@
 MESH = pl.DeviceIdType.MESH
 CORES = 2
 CHIPS = 64
+PART = 32
 RING = 4
 LEAVES = 16
 RANK = 64
@@ -111,10 +112,10 @@
     load("fo", fine_out, fo_v)
 
     def taken(row):
-        return row % 128 // 2 * 4 + (core + row // 128) % 2 * 2 + row % 2
-
-    square[...] = (taken(iota((256, 256), 0)) == iota((256, 256), 1)).astype(F32).astype(BF16)
-    wide[...] = (taken(iota((256, 512), 0)) == iota((256, 512), 1) // 2).astype(F32).astype(BF16)
+        return row % (2 * PART) // 2 * 4 + (core + row // (2 * PART)) % 2 * 2 + row % 2
+
+    square[...] = (taken(iota(square.shape, 0)) == iota(square.shape, 1)).astype(F32).astype(BF16)
+    wide[...] = (taken(iota(wide.shape, 0)) == iota(wide.shape, 1) // 2).astype(F32).astype(BF16)
 
     lane = iota((1, 128), 1)
     low = lane < RANK
@@ -156,10 +157,6 @@
     def sent(buffer, which):
         pltpu.make_async_copy(buffer, buffer, send_sem.at[which]).wait()
 
-    @pl.when((half == 1) & (core == 1))
-    def _():
-        hear_other_half()
-
     sums = [0.0, 0.0]
     for c in range(MIX_CHUNKS):
         loads["cmi", c].wait()
@@ -167,9 +164,19 @@
         sums = [sums[part] + dot(ccoef[:, span], cmi_v[part, 0, span]) for part in range(2)]
     re, im = complex_rows(*sums)
     send = jnp.concatenate([re, im], axis=0)
-    even = iota((1, 512), 1) % 2 == 0
-    send = jnp.concatenate([jnp.where(even, send, 0.0), jnp.where(even, 0.0, send)], axis=0).astype(BF16)
-    c_put[...] = dot_t(wide[...], send).astype(BF16).reshape(c_put.shape)
+    even = iota((1, 8 * PART), 1) % 2 == 0
+
+    def put(target, matrix, values):
+        for at in range(0, CHIPS, PART):
+            step = matrix.shape[1] // PART
+            part = values[:, at * step : (at + PART) * step]
+            if matrix is wide:
+                part = jnp.concatenate([jnp.where(even, part, 0.0), jnp.where(even, 0.0, part)], axis=0)
+            rows = dot_t(matrix[...], part.astype(BF16)).astype(BF16)
+            for k in range(CORES):
+                target[k, at : at + PART] = rows[k * 2 * PART : (k + 1) * 2 * PART].reshape(PART, 2, 128)
+
+    put(c_put, wide, send)
 
     def send_coarse(direct):
         for there in chips(1):
@@ -179,6 +186,10 @@
                     remote(c_put.at[k, there], target, 2 * k, 0, to)
             else:
                 remote(c_put.at[:, there], c_got.at[:, chip], 0, 1, there * CORES + core)
+
+    @pl.when((half == 1) & (core == 1))
+    def _():
+        hear_other_half()
 
     @pl.when((half == 1) & (core == 0))
     def _():
@@ -197,7 +208,7 @@
         left = fcoef[:, i * 512 : (i + 1) * 512]
         fine.extend(complex_rows(dot(left, fmi_v[0, 0, i]), dot(left, fmi_v[1, 0, i])))
     send = jnp.concatenate(fine, axis=0)
-    f_put[...] = dot_t(square[...], send.astype(BF16)).astype(BF16).reshape(f_put.shape)
+    put(f_put, square, send)
     @pl.when(core == 0)
     def _():
         pl.semaphore_wait(barrier, CORES * (CHIPS - 1) + 1)
@@ -223,13 +234,19 @@
     def _():
         send_coarse(False)
 
-    def rows_of(got, landing, which):
-        arrived(landing, which)
-        return jnp.concatenate([got[0].reshape(128, 128), landing[...].reshape(128, 128)], axis=0)
+    def columns(got, landing, matrix):
+        parts = []
+        for at in range(0, CHIPS, PART):
+            two = [got[0, at : at + PART].reshape(2 * PART, 128), landing[at : at + PART].reshape(2 * PART, 128)]
+            parts.append(dot(jnp.concatenate(two, axis=0).T, matrix[...]))
+        if matrix is wide:
+            parts = [jnp.where(even, part[:64], part[64:]) for part in parts]
+        return jnp.concatenate(parts, axis=1).astype(BF16)
 
     arrived(f_got, 1)
     remote(f_got.at[1], f_core, 3, half, chip * CORES + 1 - core)
-    got = dot(rows_of(f_got, f_core, 3).T, square[...]).astype(BF16)
+    arrived(f_core, 3)
+    got = columns(f_got, f_core, square)
     loads["fmo"].wait()
     for i in range(2):
         left = got[i * 64 : i * 64 + 64]
@@ -254,8 +271,8 @@
         arrived(c_got, 0)
         remote(c_got.at[1], c_core, 2, 1, chip * CORES + 1 - core, 4)
 
-    got = dot(rows_of(c_got, c_core, 2).T, wide[...])
-    left = jnp.where(even, got[:64], got[64:]).astype(BF16)
+    arrived(c_core, 2)
+    left = columns(c_got, c_core, wide)
     loads["cmo"].wait()
     loads["co"].wait()
     loads["fo"].wait()
@@ -306,8 +323,8 @@
             vmem(shapes[0], F32),
             *[vmem(s, BF16) for s in shapes[1:9]],
             pltpu.SMEM(shapes[9], jnp.int32),
-            vmem((256, 256), BF16),
-            vmem((256, 512), BF16),
+            vmem((4 * PART, 4 * PART), BF16),
+            vmem((4 * PART, 8 * PART), BF16),
             vmem((64, 1024), BF16),
             vmem((64, 1024), BF16),
             vmem((2, 32, 1024), F32),

time: 20.8 us -> 20.6 us (level)
  Pallas kernels: 19.8 us -> 19.5 us
    pallas_call x1, Pallas kernels: 19.8 us -> 19.5 us  [local(): pl.pallas_call(kernel, out_shape=jax.ShapeDtypeStruct(shapes[0], F32), in...]
where the time goes in v5:
time: 20.6 us; the launch traced here: 20.5 us
  Pallas kernels  19.5 us (95%)
  local copies, waits for them, and re-layouts  0.97 us (5%)
    pallas_call x1, Pallas kernels, local(): pl.pallas_call(kernel, out_shape=jax.ShapeDtypeStruct(shapes[0], F32), in...  19.5 us
    unnamed x1, local copies, waits for them, and re-layouts  0.97 us

profile of v5, /device:TPU:1, one launch (start us, length us, event | category | flops | bytes accessed | tf_op | source)
XLA Modules:
  0.0 20.5 jit_solution(7259325345280741302)
XLA Ops:
  0.0 19.5 %shard_map.100 = f32[2,32,4096]{2,1,0:T(8,128)S(1)} custom-call(f32[2,32,4096]{2,1,0:T(8,128)} %sources.1, bf16[2,16,64,256]{3,2,1,0:T(8,128)(2,1)} %coarse_in.1, bf16[2,1,1024,512]{3,2,1,0:T(8,128)(2,1)} %coarse_mix_in.1, bf16[2,1,512,1024]{3,2,1,0:T(8,128)(2,1)} %coarse_mix_out.1, bf16[2,16,64,256]{3,2,1,0:T(8,128)(2,1)} %coarse_out.1, ...), custom_call_target="tpu_custom_call" | custom-call | flops 672000000 | bytes 12582912 | tf_op jit(solution)/shard_map/pallas_call | solution.py:317
  19.5 1.0 %copy.12 = f32[2,32,4096]{2,1,0:T(8,128)} copy(f32[2,32,4096]{2,1,0:T(8,128)S(1)} %shard_map.100) | data formatting | bytes 2097152

commit v6 on v5

--- a/solution.py
+++ b/solution.py
@@ -51,7 +51,7 @@
     fine_in, fine_mix_in, fine_mix_out, fine_out, ranks,
     out,
     x_v, ci_v, cmi_v, cmo_v, co_v, fi_v, fmi_v, fmo_v, fo_v, ranks_s,
-    square, wide, ccoef, fcoef, fback,
+    square, wide, ccoef, fcoef,
     c_put, c_got, c_core, f_put, f_got, f_core,
     in_sem, send_sem, recv_sem, coarse_ok, fine_ok,
 ):
@@ -243,24 +243,36 @@
             parts = [jnp.where(even, part[:64], part[64:]) for part in parts]
         return jnp.concatenate(parts, axis=1).astype(BF16)
 
+    def row_leaves(pair, which, leaf, factor, add):
+        for n in range(2):
+            first = leaf + 2 * n
+            kept = keep(ranks_s[which, first], ranks_s[which, first + 1])
+            re, im = [jnp.where(kept, part[:, 128 * n : 128 * n + 128], 0.0) for part in pair]
+            re_other, im_other = swapped(re), swapped(im)
+            for s in (first, first + 1):
+                if s == first:
+                    rows = [jnp.where(low, re, -im_other), jnp.where(low, im, re_other)]
+                    w = jnp.concatenate([factor[0, s], factor[1, s]], axis=0)
+                else:
+                    rows = [jnp.where(low, -im_other, re), jnp.where(low, re_other, im)]
+                    w = jnp.concatenate([factor[1, s], factor[0, s]], axis=0)
+                y = dot(jnp.concatenate(rows, axis=0).astype(BF16), w).reshape(2, VECTORS, LEAF)
+                cols = slice(s * LEAF, (s + 1) * LEAF)
+                out[:, :, cols] = out[:, :, cols] + y if add else y
+
     arrived(f_got, 1)
     remote(f_got.at[1], f_core, 3, half, chip * CORES + 1 - core)
     arrived(f_core, 3)
     got = columns(f_got, f_core, square)
     loads["fmo"].wait()
+    loads["fo"].wait()
     for i in range(2):
         left = got[i * 64 : i * 64 + 64]
         for at in range(0, 512, 256):
-            re, im = complex_rows(
+            pair = complex_rows(
                 dot(left, fmo_v[0, 0, i, :, at : at + 256]), dot(left, fmo_v[1, 0, i, :, at : at + 256])
             )
-            for n in range(2):
-                place = (1 - i) * 512 + at + 128 * n
-                leaf = place // RANK
-                kept = keep(ranks_s[3, leaf], ranks_s[3, leaf + 1])
-                cols = slice(128 * n, 128 * n + 128)
-                fback[0, :, place : place + 128] = pltpu.roll(jnp.where(kept, re[:, cols], 0.0), RANK, 1)
-                fback[1, :, place : place + 128] = pltpu.roll(jnp.where(kept, im[:, cols], 0.0), RANK, 1)
+            row_leaves(pair, 3, ((1 - i) * 512 + at) // RANK, fo_v, False)
 
     @pl.when(half == 0)
     def _():
@@ -275,26 +287,9 @@
     left = columns(c_got, c_core, wide)
     loads["cmo"].wait()
     loads["co"].wait()
-    loads["fo"].wait()
     for at in range(0, 1024, 256):
         pair = complex_rows(dot(left, cmo_v[0, 0, :, at : at + 256]), dot(left, cmo_v[1, 0, :, at : at + 256]))
-        for n in range(2):
-            first = at // RANK + 2 * n
-            kept = keep(ranks_s[1, first], ranks_s[1, first + 1])
-            cr, ci = [jnp.where(kept, part[:, 128 * n : 128 * n + 128], 0.0) for part in pair]
-            cols = slice(first * RANK, first * RANK + 128)
-            fr, fi = fback[0, :, cols], fback[1, :, cols]
-            for s in (first, first + 1):
-                if s == first:
-                    re, im = jnp.where(low, cr, fr), jnp.where(low, ci, fi)
-                    two = (co_v, fo_v)
-                else:
-                    re, im = jnp.where(low, fr, cr), jnp.where(low, fi, ci)
-                    two = (fo_v, co_v)
-                rows = [jnp.concatenate([re, -im], axis=1), jnp.concatenate([im, re], axis=1)]
-                w = jnp.concatenate([two[0][0, s], two[1][0, s], two[0][1, s], two[1][1, s]], axis=0)
-                y = dot(jnp.concatenate(rows, axis=0).astype(BF16), w)
-                out[:, :, s * LEAF : (s + 1) * LEAF] = y.reshape(2, VECTORS, LEAF)
+        row_leaves(pair, 1, at // RANK, co_v, True)
 
     @pl.when(half == 0)
     def _():
@@ -327,7 +322,6 @@
             vmem((4 * PART, 8 * PART), BF16),
             vmem((64, 1024), BF16),
             vmem((64, 1024), BF16),
-            vmem((2, 32, 1024), F32),
             *[vmem(s, BF16) for s in [(CORES, CHIPS, 2, 128), (CORES, CHIPS, 2, 128), (CHIPS, 2, 128)] * 2],
             pltpu.SemaphoreType.DMA((1 + 2 * CHUNKS + MIX_CHUNKS + 6,)),
             pltpu.SemaphoreType.DMA((5,)),

time: 20.6 us -> 20.8 us (level)
  Pallas kernels: 19.5 us -> 19.8 us
    pallas_call x1, Pallas kernels: 19.5 us -> 19.8 us  [local(): pl.pallas_call(kernel, out_shape=jax.ShapeDtypeStruct(shapes[0], F32), in...]
where the time goes in v6:
time: 20.8 us
  Pallas kernels  19.8 us (95%)
  local copies, waits for them, and re-layouts  0.97 us (5%)
    pallas_call x1, Pallas kernels, local(): pl.pallas_call(kernel, out_shape=jax.ShapeDtypeStruct(shapes[0], F32), in...  19.8 us
    unnamed x1, local copies, waits for them, and re-layouts  0.97 us

profile of v6, /device:TPU:1, one launch (start us, length us, event | category | flops | bytes accessed | tf_op | source)
XLA Modules:
  0.0 20.8 jit_solution(16451982759220305888)
XLA Ops:
  0.0 19.8 %shard_map.100 = f32[2,32,4096]{2,1,0:T(8,128)S(1)} custom-call(f32[2,32,4096]{2,1,0:T(8,128)} %sources.1, bf16[2,16,64,256]{3,2,1,0:T(8,128)(2,1)} %coarse_in.1, bf16[2,1,1024,512]{3,2,1,0:T(8,128)(2,1)} %coarse_mix_in.1, bf16[2,1,512,1024]{3,2,1,0:T(8,128)(2,1)} %coarse_mix_out.1, bf16[2,16,64,256]{3,2,1,0:T(8,128)(2,1)} %coarse_out.1, ...), custom_call_target="tpu_custom_call" | custom-call | flops 672000000 | bytes 12582912 | tf_op jit(solution)/shard_map/pallas_call | solution.py:312
  19.8 1.0 %copy.12 = f32[2,32,4096]{2,1,0:T(8,128)} copy(f32[2,32,4096]{2,1,0:T(8,128)S(1)} %shard_map.100) | data formatting | bytes 2097152
